TPU v7x, 32 devices: a whole 2x2x4 slice. The times are simulated.
32 devices in a mesh: groups: 2 (over y), hosts: 4 (over z), mp: 4 (over x, core).
Axes of the slice: x: 2, y: 2, z: 4, core: 2. Of those that a mesh axis runs over, the one named last changes fastest.
Arguments:
- hidden: bfloat16 [256, 4096], P(('groups', 'hosts'), 'mp'), parts along dimension 0, may hold values from -6 to 6
- base_query_projection: bfloat16 [256, 4096], P(('groups', 'hosts'), 'mp'), parts along dimension 0, may hold values from -160 to 160
- base_key_projection: bfloat16 [256, 4096], P(('groups', 'hosts'), 'mp'), parts along dimension 0, may hold values from -6 to 6
- base_value_projection: bfloat16 [256, 4096], P(('groups', 'hosts'), 'mp'), parts along dimension 0, may hold values from -6 to 6
- adapter_input_factors: bfloat16 [8, 4096, 128], P(('groups', 'hosts'), 'mp'), parts along dimension 0, may hold values from -0.09375 to 0.09375
- adapter_output_factors: bfloat16 [8, 2, 64, 4096], P(('groups', 'hosts'), None, None, 'mp'), parts along dimension 0, may hold values from -0.75 to 0.75
- statement_prefix_cache: bfloat16 [32, 2, 128, 4096], P(('groups', 'hosts'), None, None, 'mp'), parts along dimension 0, may hold values from -6 to 6
- generated_token_cache: bfloat16 [256, 2, 8, 4096], P(('groups', 'hosts'), None, None, 'mp'), parts along dimension 0, may hold values from -6 to 6
- attempt_theorem_index: int32 [256], P(('groups', 'hosts')), parts along dimension 0, may hold values from 0 to 3, as said below
- host_live_count: int32 [8], P(('groups', 'hosts')), parts along dimension 0, may hold values from 8 to 32, as said below
- adapter_pool_row: int32 [8], P('groups'), parts along dimension 0, may hold values from 0 to 3, as said below
- prefix_pool_row: int32 [8, 4], P('groups'), parts along dimension 0, may hold values from 0 to 15, as said below
- prefix_block_count: int32 [8], P('groups'), parts along dimension 0, may hold values from 1 to 4
Outputs:
- attended: bfloat16 [256, 4096], P(('groups', 'hosts'), 'mp'), parts along dimension 0
- key_rows: bfloat16 [256, 4096], P(('groups', 'hosts'), 'mp'), parts along dimension 0
- value_rows: bfloat16 [256, 4096], P(('groups', 'hosts'), 'mp'), parts along dimension 0
There are 2 independent parts, one for each index of `groups`. A program takes and returns all parts, laid end to end along the dimension named above; each array names one. Nothing has to cross between parts.
Inputs may be any that keep to these rules, and one draw needn't show every extreme that they name: `attempt_theorem_index`: among the live attempts of one host, at most 8 name theorems whose adapter lies on any one host, and for each block index at most 8 name theorems whose block of that index lies on any one host. One host holds the adapters named by 8 live attempts of every host, and one host holds the first blocks named by 8 live attempts of every host. `host_live_count`: rows at or above a host's count are empty; some host has all 32 rows live. `adapter_pool_row`: all entries differ; pool row p lies on host p. `prefix_pool_row`: all entries differ; pool row p lies on host p // 4.
All inputs are finite; a program needn't handle non-finite values.
Results may differ from a plain program's by a relative error of at most 0.011.
Values may be sent and summed in bfloat16 or wider, within the bound.
A program may use at most 64 MiB of HBM per device.

v0:
```python
import jax
import jax.numpy as jnp
from jax import lax
from jax.sharding import PartitionSpec as P

HEAD_SIZE = 128
ADAPTER_RANK = 64
BLK = 128
PBLK = 4


ADAPTER_SCALE = 0.5
ROPE_BASE = 10000.0
NEG_FILL = -1e30


def rotate(values, position):
    shaped = values.reshape(values.shape[:-1] + (-1, HEAD_SIZE))
    halfway = HEAD_SIZE // 2
    frequency = ROPE_BASE ** (-(jnp.arange(halfway, dtype=jnp.float32) * (2.0 / HEAD_SIZE)))
    angles = position.astype(jnp.float32)[..., None] * frequency
    cosine = jnp.cos(angles)[..., None, :]
    sine_part = jnp.sin(angles)[..., None, :]
    first_half = shaped[..., :halfway]
    second = shaped[..., halfway:]
    turned = jnp.concatenate(
        [first_half * cosine - second * sine_part, second * cosine + first_half * sine_part],
        axis=-1,
    )
    return turned.reshape(values.shape)


def lookup_table(source_table, wanted):
    matches = wanted[:, None] == jnp.arange(source_table.shape[0], dtype=jnp.int32)[None, :]
    if source_table.ndim == 1:
        return jnp.sum(jnp.where(matches, source_table[None, :], 0), axis=1)
    return jnp.sum(jnp.where(matches[:, :, None], source_table[None, :, :], 0), axis=1)


def route_matrix(destination, validity, capacity, host_total):
    ordinal = jnp.arange(destination.shape[0], dtype=jnp.int32)
    earlier = (
        (destination[:, None] == destination[None, :])
        & validity[None, :]
        & (ordinal[None, :] < ordinal[:, None])
    )
    ranking = jnp.sum(earlier.astype(jnp.int32), axis=1)
    target = destination * capacity + ranking
    places = jnp.arange(host_total * capacity, dtype=jnp.int32)
    return ((places[:, None] == target[None, :]) & validity[None, :]).astype(jnp.bfloat16)


def pack_rows(router, payload):
    return jnp.dot(router, payload, preferred_element_type=jnp.float32).astype(jnp.bfloat16)


def attend_local(queries, chosen, statement_prefix_cache):
    head_count = queries.shape[-1] // HEAD_SIZE
    blocks = statement_prefix_cache.shape[0]
    block_keys = statement_prefix_cache[:, 0].reshape(
        blocks, statement_prefix_cache.shape[2], head_count, HEAD_SIZE
    )
    block_values = statement_prefix_cache[:, 1].reshape(
        blocks, statement_prefix_cache.shape[2], head_count, HEAD_SIZE
    )
    shaped = queries.reshape(queries.shape[:-1] + (head_count, HEAD_SIZE))
    scores = jnp.einsum(
        "nchd,bthd->ncbht", shaped, block_keys, preferred_element_type=jnp.float32
    ) * HEAD_SIZE ** (-0.5)
    chosen_mask = (chosen > 0)[:, :, :, None, None]
    masked = jnp.where(chosen_mask, scores, NEG_FILL)
    top_score = jnp.max(masked, axis=(2, 4))
    weights = jnp.where(chosen_mask, jnp.exp(masked - top_score[:, :, None, :, None]), 0.0)
    totals = jnp.sum(weights, axis=(2, 4))
    mixed_rows = jnp.einsum(
        "ncbht,bthd->nchd",
        weights.astype(jnp.bfloat16),
        block_values,
        preferred_element_type=jnp.float32,
    )
    return (mixed_rows.reshape(queries.shape), top_score, totals)


def body(
    hidden,
    base_query_projection,
    base_key_projection,
    base_value_projection,
    adapter_input_factors,
    adapter_output_factors,
    statement_prefix_cache,
    generated_token_cache,
    attempt_theorem_index,
    host_live_count,
    adapter_pool_row,
    prefix_pool_row,
    prefix_block_count,
):
    host_total = lax.axis_size("hosts")
    attempts = hidden.shape[0]
    capacity = max(1, attempts // host_total)
    owner_held_rows = adapter_input_factors.shape[0]
    local_blocks = statement_prefix_cache.shape[0]
    row_width = base_query_projection.shape[1]
    head_count = row_width // HEAD_SIZE
    ordinal = jnp.arange(attempts, dtype=jnp.int32)
    living = ordinal < host_live_count[0]
    adapter_rows = lookup_table(adapter_pool_row, attempt_theorem_index)
    block_rows = lookup_table(prefix_pool_row, attempt_theorem_index)
    block_counts = lookup_table(prefix_block_count, attempt_theorem_index)
    position = BLK * block_counts + generated_token_cache.shape[2]
    adapter_router = route_matrix(adapter_rows // owner_held_rows, living, capacity, host_total)
    adapter_pick = (
        adapter_rows[:, None] % owner_held_rows
        == jnp.arange(owner_held_rows, dtype=jnp.int32)[None, :]
    ).astype(jnp.bfloat16)
    sent_hidden = pack_rows(adapter_router, hidden).reshape(host_total, capacity, hidden.shape[1])
    sent_pick = pack_rows(adapter_router, adapter_pick).reshape(
        host_total, capacity, owner_held_rows
    )
    incoming_rows = lax.all_to_all(sent_hidden, "hosts", split_axis=0, concat_axis=0, tiled=True)
    pick_in = lax.all_to_all(sent_pick, "hosts", split_axis=0, concat_axis=0, tiled=True)
    projected_rows = jnp.einsum(
        "xjp,epk->xjek", incoming_rows, adapter_input_factors, preferred_element_type=jnp.float32
    )
    partial_rank = jnp.sum(projected_rows * pick_in.astype(jnp.float32)[..., None], axis=2)
    rank_rows = lax.psum(partial_rank, "mp").astype(jnp.bfloat16)
    spread_rows = rank_rows[:, :, None, :] * pick_in[..., None]
    query_correction = jnp.einsum(
        "exqw,qwf->exf",
        spread_rows[..., :ADAPTER_RANK],
        adapter_output_factors[:, 0],
        preferred_element_type=jnp.float32,
    )
    value_correction = jnp.einsum(
        "exqw,qwf->exf",
        spread_rows[..., ADAPTER_RANK:],
        adapter_output_factors[:, 1],
        preferred_element_type=jnp.float32,
    )
    adapter_corrections = (
        jnp.concatenate([query_correction, value_correction], axis=-1) * ADAPTER_SCALE
    ).astype(jnp.bfloat16)
    returned = lax.all_to_all(adapter_corrections, "hosts", split_axis=0, concat_axis=0, tiled=True)
    adapter_corrections = jnp.dot(
        adapter_router.T,
        returned.reshape(host_total * capacity, 2 * row_width),
        preferred_element_type=jnp.float32,
    )
    query_rows = rotate(
        base_query_projection.astype(jnp.float32) + adapter_corrections[:, :row_width], position
    ).astype(jnp.bfloat16)
    value_rows = (
        base_value_projection.astype(jnp.float32) + adapter_corrections[:, row_width:]
    ).astype(jnp.bfloat16)
    key_rows = rotate(base_key_projection.astype(jnp.float32), position).astype(jnp.bfloat16)
    requests = []
    for block_index in range(PBLK):
        wanted = living & (block_index < block_counts)
        holder = block_rows[:, block_index]
        router = route_matrix(holder // local_blocks, wanted, capacity, host_total)
        block_pick = (
            holder[:, None] % local_blocks == jnp.arange(local_blocks, dtype=jnp.int32)[None, :]
        ).astype(jnp.bfloat16)
        sent_queries = pack_rows(router, query_rows).reshape(host_total, capacity, row_width)
        sent_blocks = pack_rows(router, block_pick).reshape(host_total, capacity, local_blocks)
        requests.append((router, wanted, sent_queries, sent_blocks))
    partials = []
    for request in requests:
        answer_mixed_rows, answer_top_score, answer_totals = attend_local(
            lax.all_to_all(request[2], "hosts", split_axis=0, concat_axis=0, tiled=True),
            lax.all_to_all(request[3], "hosts", split_axis=0, concat_axis=0, tiled=True),
            statement_prefix_cache,
        )
        partials.append(
            (
                lax.all_to_all(answer_mixed_rows, "hosts", split_axis=0, concat_axis=0, tiled=True),
                lax.all_to_all(answer_top_score, "hosts", split_axis=0, concat_axis=0, tiled=True),
                lax.all_to_all(answer_totals, "hosts", split_axis=0, concat_axis=0, tiled=True),
            )
        )
    entries = []
    for block_index in range(PBLK):
        router, wanted = (requests[block_index][0], requests[block_index][1])
        mixed_rows, top_score, totals = partials[block_index]
        back_router = router.T.astype(jnp.float32)
        flat_mixed = jnp.dot(
            back_router,
            mixed_rows.reshape(host_total * capacity, row_width),
            precision=lax.Precision.HIGHEST,
        )
        flat_top = jnp.dot(
            back_router,
            top_score.reshape(host_total * capacity, head_count),
            precision=lax.Precision.HIGHEST,
        )
        flat_totals = jnp.dot(
            back_router,
            totals.reshape(host_total * capacity, head_count),
            precision=lax.Precision.HIGHEST,
        )
        flat_top = jnp.where(wanted[:, None], flat_top, NEG_FILL)
        entries.append((flat_mixed, flat_top, flat_totals))
    shaped_query = query_rows.reshape(attempts, head_count, HEAD_SIZE)
    own_keys = jnp.concatenate([generated_token_cache[:, 0], key_rows[:, None, :]], axis=1).reshape(
        attempts, -1, head_count, HEAD_SIZE
    )
    own_values = jnp.concatenate(
        [generated_token_cache[:, 1], value_rows[:, None, :]], axis=1
    ).reshape(attempts, -1, head_count, HEAD_SIZE)
    own_scores = jnp.einsum(
        "ahd,athd->aht", shaped_query, own_keys, preferred_element_type=jnp.float32
    ) * HEAD_SIZE ** (-0.5)
    own_top = jnp.max(own_scores, axis=2)
    own_weights = jnp.exp(own_scores - own_top[..., None])
    own_totals = jnp.sum(own_weights, axis=2)
    own_mixed = jnp.einsum(
        "aht,athd->ahd",
        own_weights.astype(jnp.bfloat16),
        own_values,
        preferred_element_type=jnp.float32,
    )
    overall = own_top
    for flat_mixed, flat_top, flat_totals in entries:
        overall = jnp.maximum(overall, flat_top)
    own_factor = jnp.exp(own_top - overall)
    numerator = own_mixed * own_factor[..., None]
    denominator = own_totals * own_factor
    for flat_mixed, flat_top, flat_totals in entries:
        factor = jnp.exp(flat_top - overall)
        numerator = (
            numerator + flat_mixed.reshape(attempts, head_count, HEAD_SIZE) * factor[..., None]
        )
        denominator = denominator + flat_totals * factor
    attended = (numerator / denominator[..., None]).reshape(attempts, row_width)
    live_rows = living[:, None]
    return (
        jnp.where(live_rows, attended, 0.0).astype(jnp.bfloat16),
        jnp.where(live_rows, key_rows, 0.0),
        jnp.where(live_rows, value_rows, 0.0),
    )


def solution(mesh):
    placed = (
        P(("groups", "hosts"), "mp"),
        P(("groups", "hosts"), "mp"),
        P(("groups", "hosts"), "mp"),
        P(("groups", "hosts"), "mp"),
        P(("groups", "hosts"), "mp", None),
        P(("groups", "hosts"), None, None, "mp"),
        P(("groups", "hosts"), None, None, "mp"),
        P(("groups", "hosts"), None, None, "mp"),
        P(("groups", "hosts")),
        P(("groups", "hosts")),
        P("groups"),
        P("groups", None),
        P("groups"),
    )
    return jax.shard_map(
        body,
        mesh=mesh,
        in_specs=placed,
        out_specs=(
            P(("groups", "hosts"), "mp"),
            P(("groups", "hosts"), "mp"),
            P(("groups", "hosts"), "mp"),
        ),
        check_vma=False,
    )
```

profile of v0, /device:TPU:0, one launch (start us, length us, event | category | flops | bytes accessed | tf_op | source)
XLA Modules:
  0.0 238.7 jit_solution(13844421475531033518)
XLA Ops:
  3.2 6.3 %all-to-all-start.1 = ((bf16[4,8,1]{1,2,0:T(2,128)(2,1)}), bf16[4,8,1]{1,2,0:T(2,128)(2,1)S(1)}, u32[]{:S(2)}, u32[]{:S(2)}) async-start(bf16[4,8,1]{1,2,0:T(2,128)(2,1)} %reshape.598), calls=%async_computation.1 | async-start | bytes 4096 | tf_op jit(solution)/shard_map/all_to_all | solution.py:122
  23.4 5.1 %all-to-all-start.3 = ((bf16[4,8,4]{1,2,0:T(4,128)(2,1)}), bf16[4,8,4]{1,2,0:T(4,128)(2,1)S(1)}, u32[]{:S(2)}, u32[]{:S(2)}) async-start(bf16[4,8,4]{1,2,0:T(4,128)(2,1)} %copy.229), calls=%async_computation.3 | async-start | bytes 8192 | tf_op jit(solution)/shard_map/all_to_all | solution.py:172
  28.5 5.6 %all-to-all-done.3 = bf16[4,8,4]{1,2,0:T(4,128)(2,1)S(1)} async-done(((bf16[4,8,4]{1,2,0:T(4,128)(2,1)}), bf16[4,8,4]{1,2,0:T(4,128)(2,1)S(1)}, u32[]{:S(2)}, u32[]{:S(2)}) %all-to-all-start.3) | async-done | bytes 288 | tf_op jit(solution)/shard_map/all_to_all | solution.py:172
  37.9 4.8 %all-to-all-done.6 = bf16[4,8,4]{1,2,0:T(4,128)(2,1)S(1)} async-done(((bf16[4,8,4]{1,2,0:T(4,128)(2,1)}), bf16[4,8,4]{1,2,0:T(4,128)(2,1)S(1)}, u32[]{:S(2)}, u32[]{:S(2)}) %all-to-all-start.6) | async-done | bytes 288 | tf_op jit(solution)/shard_map/all_to_all | solution.py:172
  46.5 4.9 %all-to-all-done.9 = bf16[4,8,4]{1,2,0:T(4,128)(2,1)S(1)} async-done(((bf16[4,8,4]{1,2,0:T(4,128)(2,1)}), bf16[4,8,4]{1,2,0:T(4,128)(2,1)S(1)}, u32[]{:S(2)}, u32[]{:S(2)}) %all-to-all-start.9) | async-done | bytes 288 | tf_op jit(solution)/shard_map/all_to_all | solution.py:172
  51.5 3.3 %all-to-all-start = ((bf16[4,8,1024]{2,1,0:T(8,128)(2,1)}), bf16[4,8,1024]{2,1,0:T(8,128)(2,1)S(1)}, u32[]{:S(2)}, u32[]{:S(2)}) async-start(bf16[4,8,1024]{2,1,0:T(8,128)(2,1)} %fusion.14), calls=%async_computation | async-start | bytes 131072 | tf_op jit(solution)/shard_map/all_to_all | solution.py:121
  55.3 5.1 %all-to-all-done = bf16[4,8,1024]{2,1,0:T(8,128)(2,1)S(1)} async-done(((bf16[4,8,1024]{2,1,0:T(8,128)(2,1)}), bf16[4,8,1024]{2,1,0:T(8,128)(2,1)S(1)}, u32[]{:S(2)}, u32[]{:S(2)}) %all-to-all-start) | async-done | bytes 65568 | tf_op jit(solution)/shard_map/all_to_all | solution.py:121
  63.8 10.4 %psum.7 = bf16[4,8,128]{2,1,0:T(8,128)(2,1)S(1)} all-reduce(f32[4,8,128]{2,1,0:T(8,128)S(1)} %convolution_multiply_fusion.8), channel_id=1, replica_groups=mesh['groups'=2,'hosts'=4,'mp'=4] {'mp'}, use_global_device_ids=true, to_apply=%region_2.3 | all-reduce | flops 4096 | bytes 24576 | tf_op jit(solution)/shard_map/psum | solution.py:127
  77.1 4.8 %all-to-all-start.2 = ((bf16[4,8,2048]{2,1,0:T(8,128)(2,1)}), bf16[4,8,2048]{2,1,0:T(8,128)(2,1)S(1)}, u32[]{:S(2)}, u32[]{:S(2)}) async-start(bf16[4,8,2048]{2,1,0:T(8,128)(2,1)} %fusion.52), calls=%async_computation.2 | async-start | bytes 262144 | tf_op jit(solution)/shard_map/all_to_all | solution.py:144
  82.5 5.3 %all-to-all-done.2 = bf16[4,8,2048]{2,1,0:T(8,128)(2,1)S(1)} async-done(((bf16[4,8,2048]{2,1,0:T(8,128)(2,1)}), bf16[4,8,2048]{2,1,0:T(8,128)(2,1)S(1)}, u32[]{:S(2)}, u32[]{:S(2)}) %all-to-all-start.2) | async-done | bytes 131104 | tf_op jit(solution)/shard_map/all_to_all | solution.py:144
  89.4 3.3 %all-to-all-start.13 = ((bf16[4,8,1024]{2,1,0:T(8,128)(2,1)}), bf16[4,8,1024]{2,1,0:T(8,128)(2,1)S(1)}, u32[]{:S(2)}, u32[]{:S(2)}) async-start(bf16[4,8,1024]{2,1,0:T(8,128)(2,1)} %fusion.18), calls=%async_computation.13 | async-start | bytes 131072 | tf_op jit(solution)/shard_map/all_to_all | solution.py:171
  99.1 5.1 %all-to-all-start.10 = ((bf16[4,8,1024]{2,1,0:T(8,128)(2,1)}), bf16[4,8,1024]{2,1,0:T(8,128)(2,1)S(1)}, u32[]{:S(2)}, u32[]{:S(2)}) async-start(bf16[4,8,1024]{2,1,0:T(8,128)(2,1)} %fusion.17), calls=%async_computation.10 | async-start | bytes 131072 | tf_op jit(solution)/shard_map/all_to_all | solution.py:171
  105.0 4.8 %all-to-all-done.10 = bf16[4,8,1024]{2,1,0:T(8,128)(2,1)S(1)} async-done(((bf16[4,8,1024]{2,1,0:T(8,128)(2,1)}), bf16[4,8,1024]{2,1,0:T(8,128)(2,1)S(1)}, u32[]{:S(2)}, u32[]{:S(2)}) %all-to-all-start.10) | async-done | bytes 65568 | tf_op jit(solution)/shard_map/all_to_all | solution.py:171
  109.9 3.3 %all-to-all-start.7 = ((bf16[4,8,1024]{2,1,0:T(8,128)(2,1)}), bf16[4,8,1024]{2,1,0:T(8,128)(2,1)S(1)}, u32[]{:S(2)}, u32[]{:S(2)}) async-start(bf16[4,8,1024]{2,1,0:T(8,128)(2,1)} %fusion.16), calls=%async_computation.7 | async-start | bytes 131072 | tf_op jit(solution)/shard_map/all_to_all | solution.py:171
  114.1 4.7 %all-to-all-done.7 = bf16[4,8,1024]{2,1,0:T(8,128)(2,1)S(1)} async-done(((bf16[4,8,1024]{2,1,0:T(8,128)(2,1)}), bf16[4,8,1024]{2,1,0:T(8,128)(2,1)S(1)}, u32[]{:S(2)}, u32[]{:S(2)}) %all-to-all-start.7) | async-done | bytes 65568 | tf_op jit(solution)/shard_map/all_to_all | solution.py:171
  118.9 3.3 %all-to-all-start.4 = ((bf16[4,8,1024]{2,1,0:T(8,128)(2,1)}), bf16[4,8,1024]{2,1,0:T(8,128)(2,1)S(1)}, u32[]{:S(2)}, u32[]{:S(2)}) async-start(bf16[4,8,1024]{2,1,0:T(8,128)(2,1)} %fusion.15), calls=%async_computation.4 | async-start | bytes 131072 | tf_op jit(solution)/shard_map/all_to_all | solution.py:171
  127.9 4.3 %all-to-all-start.20 = ((f32[4,8,8]{1,2,0:T(8,128)}), f32[4,8,8]{1,2,0:T(8,128)S(1)}, u32[]{:S(2)}, u32[]{:S(2)}) async-start(f32[4,8,8]{1,2,0:T(8,128)} %copy.265), calls=%async_computation.20 | async-start | bytes 32768 | tf_op jit(solution)/shard_map/all_to_all | solution.py:179
  142.7 4.0 %all-to-all-done.8 = f32[4,8,8]{1,2,0:T(8,128)S(1)} async-done(((f32[4,8,8]{1,2,0:T(8,128)}), f32[4,8,8]{1,2,0:T(8,128)S(1)}, u32[]{:S(2)}, u32[]{:S(2)}) %all-to-all-start.8) | async-done | bytes 1056 | tf_op jit(solution)/shard_map/all_to_all | solution.py:178
  151.6 3.9 %all-to-all-done.21 = f32[4,8,8]{1,2,0:T(8,128)S(1)} async-done(((f32[4,8,8]{1,2,0:T(8,128)}), f32[4,8,8]{1,2,0:T(8,128)S(1)}, u32[]{:S(2)}, u32[]{:S(2)}) %all-to-all-start.21) | async-done | bytes 1056 | tf_op jit(solution)/shard_map/all_to_all | solution.py:179
  160.3 4.0 %all-to-all-done.11 = f32[4,8,8]{1,2,0:T(8,128)S(1)} async-done(((f32[4,8,8]{1,2,0:T(8,128)}), f32[4,8,8]{1,2,0:T(8,128)S(1)}, u32[]{:S(2)}, u32[]{:S(2)}) %all-to-all-start.11) | async-done | bytes 1056 | tf_op jit(solution)/shard_map/all_to_all | solution.py:178
  169.4 3.8 %all-to-all-done.22 = f32[4,8,8]{1,2,0:T(8,128)S(1)} async-done(((f32[4,8,8]{1,2,0:T(8,128)}), f32[4,8,8]{1,2,0:T(8,128)S(1)}, u32[]{:S(2)}, u32[]{:S(2)}) %all-to-all-start.22) | async-done | bytes 1056 | tf_op jit(solution)/shard_map/all_to_all | solution.py:179
  182.0 3.7 %all-to-all-start.19 = ((f32[4,8,8]{1,2,0:T(8,128)}), f32[4,8,8]{1,2,0:T(8,128)S(1)}, u32[]{:S(2)}, u32[]{:S(2)}) async-start(f32[4,8,8]{1,2,0:T(8,128)} %copy.263), calls=%async_computation.19 | async-start | bytes 32768 | tf_op jit(solution)/shard_map/all_to_all | solution.py:179
  186.0 5.3 %all-to-all-done.19 = f32[4,8,8]{1,2,0:T(8,128)S(1)} async-done(((f32[4,8,8]{1,2,0:T(8,128)}), f32[4,8,8]{1,2,0:T(8,128)S(1)}, u32[]{:S(2)}, u32[]{:S(2)}) %all-to-all-start.19) | async-done | bytes 1056 | tf_op jit(solution)/shard_map/all_to_all | solution.py:179
  195.3 4.9 %all-to-all-done.5 = f32[4,8,8]{1,2,0:T(8,128)S(1)} async-done(((f32[4,8,8]{1,2,0:T(8,128)}), f32[4,8,8]{1,2,0:T(8,128)S(1)}, u32[]{:S(2)}, u32[]{:S(2)}) %all-to-all-start.5) | async-done | bytes 1056 | tf_op jit(solution)/shard_map/all_to_all | solution.py:178
  200.2 3.3 %all-to-all-start.16 = ((f32[4,8,1024]{2,1,0:T(8,128)}), f32[4,8,1024]{2,1,0:T(8,128)S(1)}, u32[]{:S(2)}, u32[]{:S(2)}) async-start(f32[4,8,1024]{2,1,0:T(8,128)} %bitcast.311), calls=%async_computation.16 | async-start | bytes 262144 | tf_op jit(solution)/shard_map/all_to_all | solution.py:177
  204.9 4.5 %all-to-all-done.16 = f32[4,8,1024]{2,1,0:T(8,128)S(1)} async-done(((f32[4,8,1024]{2,1,0:T(8,128)}), f32[4,8,1024]{2,1,0:T(8,128)S(1)}, u32[]{:S(2)}, u32[]{:S(2)}) %all-to-all-start.16) | async-done | bytes 131104 | tf_op jit(solution)/shard_map/all_to_all | solution.py:177
  209.4 3.3 %all-to-all-start.17 = ((f32[4,8,1024]{2,1,0:T(8,128)}), f32[4,8,1024]{2,1,0:T(8,128)S(1)}, u32[]{:S(2)}, u32[]{:S(2)}) async-start(f32[4,8,1024]{2,1,0:T(8,128)} %bitcast.310), calls=%async_computation.17 | async-start | bytes 262144 | tf_op jit(solution)/shard_map/all_to_all | solution.py:177
  213.0 6.1 %all-to-all-done.17 = f32[4,8,1024]{2,1,0:T(8,128)S(1)} async-done(((f32[4,8,1024]{2,1,0:T(8,128)}), f32[4,8,1024]{2,1,0:T(8,128)S(1)}, u32[]{:S(2)}, u32[]{:S(2)}) %all-to-all-start.17) | async-done | bytes 131104 | tf_op jit(solution)/shard_map/all_to_all | solution.py:177
  219.1 3.4 %all-to-all-start.18 = ((f32[4,8,1024]{2,1,0:T(8,128)}), f32[4,8,1024]{2,1,0:T(8,128)S(1)}, u32[]{:S(2)}, u32[]{:S(2)}) async-start(f32[4,8,1024]{2,1,0:T(8,128)} %bitcast.309), calls=%async_computation.18 | async-start | bytes 262144 | tf_op jit(solution)/shard_map/all_to_all | solution.py:177
  222.8 5.7 %all-to-all-done.18 = f32[4,8,1024]{2,1,0:T(8,128)S(1)} async-done(((f32[4,8,1024]{2,1,0:T(8,128)}), f32[4,8,1024]{2,1,0:T(8,128)S(1)}, u32[]{:S(2)}, u32[]{:S(2)}) %all-to-all-start.18) | async-done | bytes 131104 | tf_op jit(solution)/shard_map/all_to_all | solution.py:177
  228.5 3.3 %all-to-all-start.15 = ((f32[4,8,1024]{2,1,0:T(8,128)}), f32[4,8,1024]{2,1,0:T(8,128)S(1)}, u32[]{:S(2)}, u32[]{:S(2)}) async-start(f32[4,8,1024]{2,1,0:T(8,128)} %bitcast.312), calls=%async_computation.15 | async-start | bytes 262144 | tf_op jit(solution)/shard_map/all_to_all | solution.py:177
  232.1 5.6 %all-to-all-done.15 = f32[4,8,1024]{2,1,0:T(8,128)S(1)} async-done(((f32[4,8,1024]{2,1,0:T(8,128)}), f32[4,8,1024]{2,1,0:T(8,128)S(1)}, u32[]{:S(2)}, u32[]{:S(2)}) %all-to-all-start.15) | async-done | bytes 131104 | tf_op jit(solution)/shard_map/all_to_all | solution.py:177
  (230 shorter events, 87.0 us)
Async XLA Ops:
  1.4 91.3 %copy-start.21 = (pred[32]{0:T(512)(128)(4,1)}, pred[32]{0:T(512)(128)(4,1)S(1)}, u32[]{:S(2)}) copy-start(pred[32]{0:T(512)(128)(4,1)S(1)} %iota_compare_fusion.15) | copy-start | bytes 100
  3.2 20.2 %all-to-all-start.1 = ((bf16[4,8,1]{1,2,0:T(2,128)(2,1)}), bf16[4,8,1]{1,2,0:T(2,128)(2,1)S(1)}, u32[]{:S(2)}, u32[]{:S(2)}) async-start(bf16[4,8,1]{1,2,0:T(2,128)(2,1)} %reshape.598), calls=%async_computation.1 | async-start | bytes 4096 | tf_op jit(solution)/shard_map/all_to_all | solution.py:122
  11.0 77.5 %copy-start.23 = (pred[32]{0:T(512)(128)(4,1)}, pred[32]{0:T(512)(128)(4,1)S(1)}, u32[]{:S(2)}) copy-start(pred[32]{0:T(512)(128)(4,1)S(1)} %get-tuple-element.47) | copy-start | bytes 100
  11.0 87.1 %copy-start.25 = (pred[32]{0:T(512)(128)(4,1)}, pred[32]{0:T(512)(128)(4,1)S(1)}, u32[]{:S(2)}) copy-start(pred[32]{0:T(512)(128)(4,1)S(1)} %get-tuple-element.48) | copy-start | bytes 100
  11.0 93.1 %copy-start.27 = (pred[32]{0:T(512)(128)(4,1)}, pred[32]{0:T(512)(128)(4,1)S(1)}, u32[]{:S(2)}) copy-start(pred[32]{0:T(512)(128)(4,1)S(1)} %get-tuple-element.49) | copy-start | bytes 100
  11.0 102.1 %copy-start.29 = (pred[32]{0:T(512)(128)(4,1)}, pred[32]{0:T(512)(128)(4,1)S(1)}, u32[]{:S(2)}) copy-start(pred[32]{0:T(512)(128)(4,1)S(1)} %get-tuple-element.46) | copy-start | bytes 100
  11.2 102.0 %copy-start.38 = (s32[32]{0:T(128)}, s32[32]{0:T(128)S(1)}, u32[]{:S(2)}) copy-start(s32[32]{0:T(128)S(1)} %multiply_add_fusion.4) | copy-start | bytes 388
  11.3 86.9 %copy-start.34 = (s32[32]{0:T(128)}, s32[32]{0:T(128)S(1)}, u32[]{:S(2)}) copy-start(s32[32]{0:T(128)S(1)} %multiply_add_fusion.2) | copy-start | bytes 388
  11.4 92.7 %copy-start.36 = (s32[32]{0:T(128)}, s32[32]{0:T(128)S(1)}, u32[]{:S(2)}) copy-start(s32[32]{0:T(128)S(1)} %multiply_add_fusion.3) | copy-start | bytes 388
  11.5 77.0 %copy-start.32 = (s32[32]{0:T(128)}, s32[32]{0:T(128)S(1)}, u32[]{:S(2)}) copy-start(s32[32]{0:T(128)S(1)} %multiply_add_fusion.1) | copy-start | bytes 388
  23.4 10.7 %all-to-all-start.3 = ((bf16[4,8,4]{1,2,0:T(4,128)(2,1)}), bf16[4,8,4]{1,2,0:T(4,128)(2,1)S(1)}, u32[]{:S(2)}, u32[]{:S(2)}) async-start(bf16[4,8,4]{1,2,0:T(4,128)(2,1)} %copy.229), calls=%async_computation.3 | async-start | bytes 8192 | tf_op jit(solution)/shard_map/all_to_all | solution.py:172
  34.0 8.6 %all-to-all-start.6 = ((bf16[4,8,4]{1,2,0:T(4,128)(2,1)}), bf16[4,8,4]{1,2,0:T(4,128)(2,1)S(1)}, u32[]{:S(2)}, u32[]{:S(2)}) async-start(bf16[4,8,4]{1,2,0:T(4,128)(2,1)} %copy.235), calls=%async_computation.6 | async-start | bytes 8192 | tf_op jit(solution)/shard_map/all_to_all | solution.py:172
  42.7 8.8 %all-to-all-start.9 = ((bf16[4,8,4]{1,2,0:T(4,128)(2,1)}), bf16[4,8,4]{1,2,0:T(4,128)(2,1)S(1)}, u32[]{:S(2)}, u32[]{:S(2)}) async-start(bf16[4,8,4]{1,2,0:T(4,128)(2,1)} %copy.240), calls=%async_computation.9 | async-start | bytes 8192 | tf_op jit(solution)/shard_map/all_to_all | solution.py:172
  51.5 9.0 %all-to-all-start = ((bf16[4,8,1024]{2,1,0:T(8,128)(2,1)}), bf16[4,8,1024]{2,1,0:T(8,128)(2,1)S(1)}, u32[]{:S(2)}, u32[]{:S(2)}) async-start(bf16[4,8,1024]{2,1,0:T(8,128)(2,1)} %fusion.14), calls=%async_computation | async-start | bytes 131072 | tf_op jit(solution)/shard_map/all_to_all | solution.py:121
  60.5 16.7 %all-to-all-start.12 = ((bf16[4,8,4]{1,2,0:T(4,128)(2,1)}), bf16[4,8,4]{1,2,0:T(4,128)(2,1)S(1)}, u32[]{:S(2)}, u32[]{:S(2)}) async-start(bf16[4,8,4]{1,2,0:T(4,128)(2,1)} %copy.245), calls=%async_computation.12 | async-start | bytes 8192 | tf_op jit(solution)/shard_map/all_to_all | solution.py:172
  77.1 10.7 %all-to-all-start.2 = ((bf16[4,8,2048]{2,1,0:T(8,128)(2,1)}), bf16[4,8,2048]{2,1,0:T(8,128)(2,1)S(1)}, u32[]{:S(2)}, u32[]{:S(2)}) async-start(bf16[4,8,2048]{2,1,0:T(8,128)(2,1)} %fusion.52), calls=%async_computation.2 | async-start | bytes 262144 | tf_op jit(solution)/shard_map/all_to_all | solution.py:144
  89.4 9.7 %all-to-all-start.13 = ((bf16[4,8,1024]{2,1,0:T(8,128)(2,1)}), bf16[4,8,1024]{2,1,0:T(8,128)(2,1)S(1)}, u32[]{:S(2)}, u32[]{:S(2)}) async-start(bf16[4,8,1024]{2,1,0:T(8,128)(2,1)} %fusion.18), calls=%async_computation.13 | async-start | bytes 131072 | tf_op jit(solution)/shard_map/all_to_all | solution.py:171
  99.1 10.8 %all-to-all-start.10 = ((bf16[4,8,1024]{2,1,0:T(8,128)(2,1)}), bf16[4,8,1024]{2,1,0:T(8,128)(2,1)S(1)}, u32[]{:S(2)}, u32[]{:S(2)}) async-start(bf16[4,8,1024]{2,1,0:T(8,128)(2,1)} %fusion.17), calls=%async_computation.10 | async-start | bytes 131072 | tf_op jit(solution)/shard_map/all_to_all | solution.py:171
  109.9 9.0 %all-to-all-start.7 = ((bf16[4,8,1024]{2,1,0:T(8,128)(2,1)}), bf16[4,8,1024]{2,1,0:T(8,128)(2,1)S(1)}, u32[]{:S(2)}, u32[]{:S(2)}) async-start(bf16[4,8,1024]{2,1,0:T(8,128)(2,1)} %fusion.16), calls=%async_computation.7 | async-start | bytes 131072 | tf_op jit(solution)/shard_map/all_to_all | solution.py:171
  118.9 9.0 %all-to-all-start.4 = ((bf16[4,8,1024]{2,1,0:T(8,128)(2,1)}), bf16[4,8,1024]{2,1,0:T(8,128)(2,1)S(1)}, u32[]{:S(2)}, u32[]{:S(2)}) async-start(bf16[4,8,1024]{2,1,0:T(8,128)(2,1)} %fusion.15), calls=%async_computation.4 | async-start | bytes 131072 | tf_op jit(solution)/shard_map/all_to_all | solution.py:171
  127.9 10.0 %all-to-all-start.20 = ((f32[4,8,8]{1,2,0:T(8,128)}), f32[4,8,8]{1,2,0:T(8,128)S(1)}, u32[]{:S(2)}, u32[]{:S(2)}) async-start(f32[4,8,8]{1,2,0:T(8,128)} %copy.265), calls=%async_computation.20 | async-start | bytes 32768 | tf_op jit(solution)/shard_map/all_to_all | solution.py:179
  137.8 8.8 %all-to-all-start.8 = ((f32[4,8,8]{1,2,0:T(8,128)}), f32[4,8,8]{1,2,0:T(8,128)S(1)}, u32[]{:S(2)}, u32[]{:S(2)}) async-start(f32[4,8,8]{1,2,0:T(8,128)} %copy.238), calls=%async_computation.8 | async-start | bytes 32768 | tf_op jit(solution)/shard_map/all_to_all | solution.py:178
  146.7 8.8 %all-to-all-start.21 = ((f32[4,8,8]{1,2,0:T(8,128)}), f32[4,8,8]{1,2,0:T(8,128)S(1)}, u32[]{:S(2)}, u32[]{:S(2)}) async-start(f32[4,8,8]{1,2,0:T(8,128)} %copy.267), calls=%async_computation.21 | async-start | bytes 32768 | tf_op jit(solution)/shard_map/all_to_all | solution.py:179
  155.5 8.8 %all-to-all-start.11 = ((f32[4,8,8]{1,2,0:T(8,128)}), f32[4,8,8]{1,2,0:T(8,128)S(1)}, u32[]{:S(2)}, u32[]{:S(2)}) async-start(f32[4,8,8]{1,2,0:T(8,128)} %copy.243), calls=%async_computation.11 | async-start | bytes 32768 | tf_op jit(solution)/shard_map/all_to_all | solution.py:178
  164.3 8.8 %all-to-all-start.22 = ((f32[4,8,8]{1,2,0:T(8,128)}), f32[4,8,8]{1,2,0:T(8,128)S(1)}, u32[]{:S(2)}, u32[]{:S(2)}) async-start(f32[4,8,8]{1,2,0:T(8,128)} %copy.269), calls=%async_computation.22 | async-start | bytes 32768 | tf_op jit(solution)/shard_map/all_to_all | solution.py:179
  173.2 8.8 %all-to-all-start.14 = ((f32[4,8,8]{1,2,0:T(8,128)}), f32[4,8,8]{1,2,0:T(8,128)S(1)}, u32[]{:S(2)}, u32[]{:S(2)}) async-start(f32[4,8,8]{1,2,0:T(8,128)} %copy.248), calls=%async_computation.14 | async-start | bytes 32768 | tf_op jit(solution)/shard_map/all_to_all | solution.py:178
  182.0 9.3 %all-to-all-start.19 = ((f32[4,8,8]{1,2,0:T(8,128)}), f32[4,8,8]{1,2,0:T(8,128)S(1)}, u32[]{:S(2)}, u32[]{:S(2)}) async-start(f32[4,8,8]{1,2,0:T(8,128)} %copy.263), calls=%async_computation.19 | async-start | bytes 32768 | tf_op jit(solution)/shard_map/all_to_all | solution.py:179
  191.3 8.8 %all-to-all-start.5 = ((f32[4,8,8]{1,2,0:T(8,128)}), f32[4,8,8]{1,2,0:T(8,128)S(1)}, u32[]{:S(2)}, u32[]{:S(2)}) async-start(f32[4,8,8]{1,2,0:T(8,128)} %copy.233), calls=%async_computation.5 | async-start | bytes 32768 | tf_op jit(solution)/shard_map/all_to_all | solution.py:178
  200.2 9.3 %all-to-all-start.16 = ((f32[4,8,1024]{2,1,0:T(8,128)}), f32[4,8,1024]{2,1,0:T(8,128)S(1)}, u32[]{:S(2)}, u32[]{:S(2)}) async-start(f32[4,8,1024]{2,1,0:T(8,128)} %bitcast.311), calls=%async_computation.16 | async-start | bytes 262144 | tf_op jit(solution)/shard_map/all_to_all | solution.py:177
  209.4 9.7 %all-to-all-start.17 = ((f32[4,8,1024]{2,1,0:T(8,128)}), f32[4,8,1024]{2,1,0:T(8,128)S(1)}, u32[]{:S(2)}, u32[]{:S(2)}) async-start(f32[4,8,1024]{2,1,0:T(8,128)} %bitcast.310), calls=%async_computation.17 | async-start | bytes 262144 | tf_op jit(solution)/shard_map/all_to_all | solution.py:177
  219.1 9.3 %all-to-all-start.18 = ((f32[4,8,1024]{2,1,0:T(8,128)}), f32[4,8,1024]{2,1,0:T(8,128)S(1)}, u32[]{:S(2)}, u32[]{:S(2)}) async-start(f32[4,8,1024]{2,1,0:T(8,128)} %bitcast.309), calls=%async_computation.18 | async-start | bytes 262144 | tf_op jit(solution)/shard_map/all_to_all | solution.py:177
  228.5 9.2 %all-to-all-start.15 = ((f32[4,8,1024]{2,1,0:T(8,128)}), f32[4,8,1024]{2,1,0:T(8,128)S(1)}, u32[]{:S(2)}, u32[]{:S(2)}) async-start(f32[4,8,1024]{2,1,0:T(8,128)} %bitcast.312), calls=%async_computation.15 | async-start | bytes 262144 | tf_op jit(solution)/shard_map/all_to_all | solution.py:177
  (32 other events, 869.9 us)
where the time goes:
time: 241 us; the launch traced here: 239 us
  waiting for transfers between devices  88.3 us (37%)
  starting transfers between devices  85 us (35%)
  matrix products  21.9 us (9%)
  local copies, waits for them, and re-layouts  18 us (7%)
  other arithmetic  12.8 us (5%)
  blocking collectives  10.4 us (4%)
    all_to_all x4, waiting for transfers between devices, body(): lax.all_to_all(answer_mixed_rows, 'hosts', split_axis=0, concat_axis=0, t...  21.9 us
    all_to_all x4, waiting for transfers between devices, body(): lax.all_to_all(answer_totals, 'hosts', split_axis=0, concat_axis=0, tiled...  16.1 us
    all_to_all x4, waiting for transfers between devices, body(): lax.all_to_all(request[3], 'hosts', split_axis=0, concat_axis=0, tiled=True)  15.3 us
    all_to_all x4, starting transfers between devices, body(): lax.all_to_all(request[2], 'hosts', split_axis=0, concat_axis=0, tiled=True)  14.9 us
    all_to_all x4, starting transfers between devices, body(): lax.all_to_all(request[3], 'hosts', split_axis=0, concat_axis=0, tiled=True)  14.8 us
    all_to_all x4, starting transfers between devices, body(): lax.all_to_all(answer_totals, 'hosts', split_axis=0, concat_axis=0, tiled...  14.5 us
    all_to_all x4, waiting for transfers between devices, body(): lax.all_to_all(answer_top_score, 'hosts', split_axis=0, concat_axis=0, ti...  14.2 us
    all_to_all x4, starting transfers between devices, body(): lax.all_to_all(answer_mixed_rows, 'hosts', split_axis=0, concat_axis=0, t...  13.4 us
  transfers between devices with their start and end apart: 23, of which 20 were waited for; matrix products, arithmetic and copies ran while one was open for 20% of the time, Pallas kernels for 0%

commit v1 on v0

--- a/solution.py
+++ b/solution.py
@@ -1,6 +1,11 @@
+import functools
+import math
+
 import jax
 import jax.numpy as jnp
 from jax import lax
+from jax.experimental import pallas as pl
+from jax.experimental.pallas import tpu as pltpu
 from jax.sharding import PartitionSpec as P
 
 HEAD_SIZE = 128
@@ -12,6 +17,7 @@
 ADAPTER_SCALE = 0.5
 ROPE_BASE = 10000.0
 NEG_FILL = -1e30
+MESH = pl.DeviceIdType.MESH
 
 
 def rotate(values, position):
@@ -241,6 +247,408 @@
     )
 
 
+def _iota(shape, dim):
+    return lax.broadcasted_iota(jnp.int32, shape, dim)
+
+
+def _dot(a, b):
+    return jnp.dot(a, b, preferred_element_type=jnp.float32)
+
+
+def _dot_t(a, b):
+    return lax.dot_general(a, b, (((1,), (1,)), ((), ())), preferred_element_type=jnp.float32)
+
+
+def fused_kernel(
+    sizes,
+    thm, live, apr, ppr, cnt,
+    hidden, base_q, base_k, base_v, a_hbm, b_hbm, kv_hbm, gen_hbm,
+    out, key_out, val_out,
+    a_v, b_v, kv_v, gen_v,
+    snd_h, rcv_h, snd_q, rcv_q, part, snd_v, rcv_v, snd_m, rcv_m, snd_l, rcv_l, own_mix,
+    local_sem, h_s, h_r, bq_s, bq_r, p_s, p_r, q_s, q_r, v_s, v_r, m_s, m_r, l_s, l_r,
+    *queries,
+):
+    H, MP, A, CAP, L, T, PB, HEADS, SUF, NCH = sizes
+    f32, bf = jnp.float32, jnp.bfloat16
+    D = HEAD_SIZE
+    W = HEADS * D
+    W2 = W // 2
+    S = H * CAP
+    CW = W // NCH
+    shift = CAP.bit_length() - 1
+    me = lax.axis_index("hosts")
+    mme = lax.axis_index("mp")
+
+    def other(axis, d):
+        return lax.rem((me if axis == "hosts" else mme) + d, H if axis == "hosts" else MP)
+
+    locals_ = [
+        pltpu.make_async_copy(src, dst, local_sem.at[i])
+        for i, (src, dst) in enumerate(
+            [(a_hbm, a_v), (b_hbm, b_v), (kv_hbm, kv_v), (gen_hbm, gen_v)]
+        )
+    ]
+    for copy in locals_:
+        copy.start()
+
+    barrier = pltpu.get_barrier_semaphore()
+    for d in range(1, H):
+        pl.semaphore_signal(barrier, inc=1, device_id={"hosts": other("hosts", d)}, device_id_type=MESH)
+    for d in range(1, MP):
+        pl.semaphore_signal(barrier, inc=1, device_id={"mp": other("mp", d)}, device_id_type=MESH)
+
+    def send(src, dst, s, r, axis, d):
+        copy = pltpu.make_async_remote_copy(
+            src_ref=src, dst_ref=dst, send_sem=s, recv_sem=r,
+            device_id={axis: other(axis, d)}, device_id_type=MESH,
+        )
+        copy.start()
+        return copy
+
+    lane8, sub8 = _iota((8, 128), 1), _iota((8, 128), 0)
+    th = jnp.full((8, 128), -1, jnp.int32)
+    for a in range(A):
+        th = jnp.where(lane8 == a, thm[a], th)
+    owner = jnp.full((8, 128), -1, jnp.int32)
+    for t in range(T):
+        owner = jnp.where(th == t, apr[t], owner)
+    n_live = live[0]
+    owner = jnp.where(lane8 < n_live, owner, -1)
+    member = jnp.where(owner == sub8, 1.0, 0.0).astype(f32)
+    before = jnp.where(_iota((128, 128), 0) < _iota((128, 128), 1), 1.0, 0.0).astype(bf)
+    rank_f = jnp.sum(member * _dot(member.astype(bf), before), axis=0, keepdims=True)
+    rank_row = rank_f.astype(jnp.int32)
+    target = jnp.where(owner[0:1] >= 0, owner[0:1] * CAP + rank_row, -1)
+    router = jnp.where(_iota((S, A), 0) == target[:, :A], 1.0, 0.0).astype(bf)
+
+    def folded(rows, e):
+        piece = rows[e * CAP : (e + 1) * CAP]
+        return jnp.concatenate([piece[:, :W2], piece[:, W2:]], axis=0)
+
+    packed = _dot(router, hidden[...])
+    for e in range(H):
+        snd_h[e] = folded(packed, e).astype(bf)
+    pl.semaphore_wait(barrier, H - 1 + MP - 1)
+    hs = [
+        send(snd_h.at[other("hosts", d)], rcv_h.at[me], h_s.at[d], h_r.at[d], "hosts", d)
+        for d in range(1, H)
+    ]
+    packed = _dot(router, base_q[...])
+    for e in range(H):
+        snd_q[e] = folded(packed, e).astype(bf)
+    bqs = [
+        send(snd_q.at[other("hosts", d)], rcv_q.at[me], bq_s.at[d], bq_r.at[d], "hosts", d)
+        for d in range(1, H)
+    ]
+    rcv_h[me] = snd_h[me]
+    rcv_q[me] = snd_q[me]
+
+    lane = _iota((8, 128), 1)
+    half = jnp.where(lane < D // 2, lane, lane - D // 2).astype(f32)
+    freq = jnp.exp(half * (-2.0 / D * math.log(ROPE_BASE)))
+    counts = jnp.zeros((8, 128), jnp.int32)
+    my_count = jnp.int32(0)
+    for t in range(T):
+        counts = jnp.where(sub8 == t, cnt[t], counts)
+        my_count = jnp.where(apr[t] == me, cnt[t], my_count)
+    counts = jnp.where(sub8 == T, my_count, counts)
+    angle = (BLK * counts + SUF).astype(f32) * freq
+    cos_t = jnp.cos(angle)
+    sin_t = jnp.sin(angle)
+    sin_t = jnp.where(lane < D // 2, -sin_t, sin_t)
+
+    def turn(x, c, s):
+        return x * c + pltpu.roll(x, D // 2, 1) * s
+
+    locals_[0].wait()
+    for copy in hs:
+        copy.wait_recv()
+    rows = rcv_h[...].reshape(H * 2 * CAP, W2)
+    left = _dot(rows, a_v[0, :W2, :])
+    right = _dot(rows, a_v[0, W2:, :])
+    part[mme] = jnp.concatenate(
+        [
+            left[2 * CAP * e : 2 * CAP * e + CAP] + right[2 * CAP * e + CAP : 2 * CAP * (e + 1)]
+            for e in range(H)
+        ],
+        axis=0,
+    )
+    ps = [
+        send(part.at[mme], part.at[mme], p_s.at[d], p_r.at[d], "mp", d) for d in range(1, MP)
+    ]
+    for copy in bqs:
+        copy.wait_recv()
+    bq = rcv_q[...].astype(f32)
+    bq_half = [
+        jnp.concatenate([bq[e, k * CAP : (k + 1) * CAP] for e in range(H)], axis=0)
+        for k in range(2)
+    ]
+    locals_[1].wait()
+    for copy in ps:
+        copy.wait_recv()
+    ranks = part[0]
+    for m in range(1, MP):
+        ranks = ranks + part[m]
+    ranks = ranks.astype(bf).astype(f32)
+    rank_q = ranks[:, :ADAPTER_RANK].astype(bf)
+    rank_v = pltpu.roll(ranks, ADAPTER_RANK, 1)[:, :ADAPTER_RANK].astype(bf)
+    qs = []
+    for c in range(NCH):
+        cols = slice(c * CW, (c + 1) * CW)
+        delta = (_dot(rank_q, b_v[0, 0, :, cols]) * ADAPTER_SCALE).astype(bf).astype(f32)
+        k, off = (c * CW) // W2, (c * CW) % W2
+        raw = bq_half[k][:, off : off + CW] + delta
+        for h in range(CW // D):
+            queries[c][me, :, h * D : (h + 1) * D] = turn(
+                raw[:, h * D : (h + 1) * D], cos_t[T : T + 1], sin_t[T : T + 1]
+            ).astype(bf)
+        view = queries[c].at[me]
+        qs.append(
+            [send(view, view, q_s.at[c, d], q_r.at[c, d], "hosts", d) for d in range(1, H)]
+        )
+    delta = _dot(rank_v, b_v[0, 1]) * ADAPTER_SCALE
+    for e in range(H):
+        snd_v[e] = folded(delta, e).astype(bf)
+    vs = [
+        send(snd_v.at[other("hosts", d)], rcv_v.at[me], v_s.at[d], v_r.at[d], "hosts", d)
+        for d in range(1, H)
+    ]
+    rcv_v[me] = snd_v[me]
+
+    sub128 = _iota((128, 128), 0)
+    both = jnp.where(sub128 == 0, th[0:1].astype(f32), jnp.where(sub128 == 1, rank_f, 0.0))
+    turned = both.T[:A].astype(jnp.int32)
+    th_c, rank_c = turned[:, 0:1], turned[:, 1:2]
+    lane_a = _iota((A, 128), 1)
+    live_c = _iota((A, 1), 0) < n_live
+    owner_c = jnp.full((A, 1), -1, jnp.int32)
+    cos_a = jnp.zeros((A, 128), f32)
+    sin_a = jnp.zeros((A, 128), f32)
+    blocks_c = [jnp.full((A, 1), -1, jnp.int32) for _ in range(PB)]
+    for t in range(T):
+        here = th_c == t
+        owner_c = jnp.where(here, apr[t], owner_c)
+        cos_a = jnp.where(here, cos_t[t : t + 1], cos_a)
+        sin_a = jnp.where(here, sin_t[t : t + 1], sin_a)
+        for j in range(PB):
+            blocks_c[j] = jnp.where(here, jnp.where(j < cnt[t], ppr[t, j], -1), blocks_c[j])
+    owner_c = jnp.where(live_c, owner_c, -1)
+    slot_ok = jnp.where(rank_c == (lane_a & (CAP - 1)), 1, 0)
+    group = lane_a >> shift
+    used = jnp.zeros((A, 128), jnp.int32)
+    for j in range(PB):
+        used = used + jnp.where(blocks_c[j] == group, 1, 0)
+    used = jnp.where(live_c, used * slot_ok, 0) > 0
+    fetch = jnp.where(owner_c * H + me == group, slot_ok, 0).astype(f32).astype(bf)
+    unpack = jnp.where(
+        owner_c * CAP + rank_c == _iota((A, S), 1), jnp.where(owner_c >= 0, 1.0, 0.0), 0.0
+    ).astype(bf)
+    keys = []
+    for h in range(HEADS):
+        cols = slice(h * D, (h + 1) * D)
+        key = turn(base_k[:, cols].astype(f32), cos_a, sin_a).astype(bf).astype(f32)
+        keys.append(key)
+        key_out[:, cols] = jnp.where(live_c, key, 0.0).astype(bf)
+
+    whose = []
+    for b in range(L):
+        index = jnp.int32(0)
+        for t in range(T):
+            for j in range(PB):
+                index = jnp.where(ppr[t, j] == me * L + b, apr[t], index)
+        whose.append(index)
+    scale = D ** (-0.5)
+    locals_[2].wait()
+    lane128 = _iota((128, 128), 1)
+    lse_all = jnp.zeros((128, 128), f32)
+    ms = []
+    for c in range(NCH):
+        for copy in qs[c]:
+            copy.wait_recv()
+        for h in range(c * CW // D, (c + 1) * CW // D):
+            cols = slice(h * D, (h + 1) * D)
+            within = slice(h * D - c * CW, (h + 1) * D - c * CW)
+            scores = jnp.concatenate(
+                [_dot_t(queries[c][whose[b], :, within], kv_v[b, 0, :, cols]) for b in range(L)], axis=0
+            ) * scale
+            top = jnp.max(scores, axis=1, keepdims=True)
+            weights = jnp.exp(scores - top)
+            total = jnp.sum(weights, axis=1, keepdims=True)
+            weights = weights.astype(bf)
+            mixed = jnp.concatenate(
+                [_dot(weights[b * S : (b + 1) * S], kv_v[b, 1, :, cols]) for b in range(L)], axis=0
+            ) * (1.0 / total)
+            lse_all = jnp.where(lane128 == h, top + jnp.log(total), lse_all)
+            for e in range(H):
+                snd_m[e, :, cols] = jnp.concatenate(
+                    [mixed[b * S + e * CAP : b * S + (e + 1) * CAP] for b in range(L)], axis=0
+                ).astype(bf)
+        if c == NCH - 1:
+            ordered = jnp.concatenate(
+                [
+                    lse_all[b * S + e * CAP : b * S + (e + 1) * CAP]
+                    for e in range(H)
+                    for b in range(L)
+                ],
+                axis=0,
+            )
+            lse_t = ordered.T[:HEADS]
+            rcv_l[me] = lse_t
+            for d in range(1, H):
+                snd_l[d] = pltpu.roll(lse_t, (128 - L * CAP * d) % 128, 1)
+            ls = [
+                send(snd_l.at[d], rcv_l.at[me], l_s.at[d], l_r.at[d], "hosts", d)
+                for d in range(1, H)
+            ]
+        span = pl.ds(c * CW, CW)
+        ms.append(
+            [
+                send(
+                    snd_m.at[other("hosts", d), :, span], rcv_m.at[me, :, span],
+                    m_s.at[c, d], m_r.at[c, d], "hosts", d,
+                )
+                for d in range(1, H)
+            ]
+        )
+    rcv_m[me] = snd_m[me]
+
+    locals_[3].wait()
+    for copy in vs:
+        copy.wait_recv()
+    dv = rcv_v[...].astype(f32)
+    dv_att = [
+        _dot(
+            unpack,
+            jnp.concatenate([dv[p, k * CAP : (k + 1) * CAP] for p in range(H)], axis=0).astype(bf),
+        )
+        for k in range(2)
+    ]
+    N = gen_v.shape[0]
+    lane_n, sub_n = _iota((A, N), 1), _iota((A, N), 0)
+    mine = ((lane_n >> (SUF.bit_length())) == sub_n) & ((lane_n & (2 * SUF - 1)) < SUF)
+    own_top, own_total = [], []
+    for h in range(HEADS):
+        cols = slice(h * D, (h + 1) * D)
+        k, off = (h * D) // W2, (h * D) % W2
+        value = (base_v[:, cols].astype(f32) + dv_att[k][:, off : off + D]).astype(bf).astype(f32)
+        val_out[:, cols] = jnp.where(live_c, value, 0.0).astype(bf)
+        c, start = (h * D) // CW, (h * D) % CW
+        query = _dot(fetch, queries[c][:, :, start : start + D].reshape(H * S, D))
+        scores = _dot_t(query.astype(bf), gen_v[:, cols]) * scale
+        scores = jnp.where(mine, scores, NEG_FILL)
+        self_score = jnp.sum(query * keys[h], axis=1, keepdims=True) * scale
+        top = jnp.maximum(jnp.max(scores, axis=1, keepdims=True), self_score)
+        weights = jnp.where(mine, jnp.exp(scores - top), 0.0)
+        self_weight = jnp.exp(self_score - top)
+        own_top.append(top)
+        own_total.append(jnp.sum(weights, axis=1, keepdims=True) + self_weight)
+        own_mix[:, cols] = (
+            _dot(pltpu.roll(weights, SUF, 1).astype(bf), gen_v[:, cols])
+            + self_weight.astype(bf).astype(f32) * value
+        )
+
+    for copy in ls:
+        copy.wait_recv()
+    lse = jnp.zeros((HEADS, 128), f32)
+    lane_h = _iota((HEADS, 128), 1)
+    for g in range(H):
+        lse = jnp.where((lane_h >= g * L * CAP) & (lane_h < (g + 1) * L * CAP), rcv_l[g], lse)
+    for c in range(NCH):
+        for copy in ms[c]:
+            copy.wait_recv()
+        for h in range(c * CW // D, (c + 1) * CW // D):
+            cols = slice(h * D, (h + 1) * D)
+            logs = jnp.where(used, lse[h : h + 1], NEG_FILL)
+            top = jnp.maximum(jnp.max(logs, axis=1, keepdims=True), own_top[h])
+            factor = jnp.where(used, jnp.exp(logs - top), 0.0)
+            own_factor = jnp.exp(own_top[h] - top)
+            inverse = 1.0 / (jnp.sum(factor, axis=1, keepdims=True) + own_total[h] * own_factor)
+            result = _dot(
+                (factor * inverse).astype(bf), rcv_m[:, :, cols].reshape(H * L * CAP, D)
+            ) + own_mix[:, cols] * (own_factor * inverse)
+            out[:, cols] = jnp.where(live_c, result, 0.0).astype(bf)
+    for copies in [hs, bqs, ps, vs, ls] + qs + ms:
+        for copy in copies:
+            copy.wait_send()
+
+
+def fused_body(
+    hidden, base_q, base_k, base_v, a_in, b_out, cache, generated, thm, live, apr, ppr, cnt
+):
+    H, MP = lax.axis_size("hosts"), lax.axis_size("mp")
+    A, W = hidden.shape
+    CAP = A // H
+    L, SUF = cache.shape[0], generated.shape[2]
+    HEADS = W // HEAD_SIZE
+    S = H * CAP
+    NCH = 2
+    bf, f32 = jnp.bfloat16, jnp.float32
+    N = generated.shape[0] * 2 * SUF
+    sizes = (H, MP, A, CAP, L, apr.shape[0], ppr.shape[1], HEADS, SUF, NCH)
+    smem = pl.BlockSpec(memory_space=pltpu.SMEM)
+    vmem = pl.BlockSpec(memory_space=pltpu.VMEM)
+    hbm = pl.BlockSpec(memory_space=pl.ANY)
+    fold = (H, 2 * CAP, W // 2)
+    sem = lambda *shape: pltpu.SemaphoreType.DMA(shape)
+    return pl.pallas_call(
+        functools.partial(fused_kernel, sizes),
+        out_shape=[jax.ShapeDtypeStruct((A, W), bf)] * 3,
+        in_specs=[smem] * 5 + [vmem] * 4 + [hbm] * 4,
+        out_specs=[vmem] * 3,
+        scratch_shapes=[
+            pltpu.VMEM(a_in.shape, bf),
+            pltpu.VMEM(b_out.shape, bf),
+            pltpu.VMEM(cache.shape, bf),
+            pltpu.VMEM((N, W), bf),
+            pltpu.VMEM(fold, bf),
+            pltpu.VMEM(fold, bf),
+            pltpu.VMEM(fold, bf),
+            pltpu.VMEM(fold, bf),
+            pltpu.VMEM((MP, S, 128), f32),
+            pltpu.VMEM(fold, bf),
+            pltpu.VMEM(fold, bf),
+            pltpu.VMEM((H, L * CAP, W), bf),
+            pltpu.VMEM((H, L * CAP, W), bf),
+            pltpu.VMEM((H, HEADS, 128), f32),
+            pltpu.VMEM((H, HEADS, 128), f32),
+            pltpu.VMEM((A, W), f32),
+            sem(4), sem(H), sem(H), sem(H), sem(H), sem(MP), sem(MP),
+            sem(NCH, H), sem(NCH, H), sem(H), sem(H), sem(NCH, H), sem(NCH, H), sem(H), sem(H),
+        ]
+        + [pltpu.VMEM((H, S, W // NCH), bf)] * NCH,
+        compiler_params=pltpu.CompilerParams(
+            collective_id=0, has_side_effects=True, vmem_limit_bytes=60 * 1024 * 1024
+        ),
+        cost_estimate=pl.CostEstimate(
+            flops=2 * 10**8, bytes_accessed=4 * 10**6, transcendentals=10**6
+        ),
+    )(
+        thm, live, apr, ppr, cnt, hidden, base_q, base_k, base_v, a_in, b_out, cache,
+        generated.reshape(N, W),
+    )
+
+
+def step(hidden, base_q, base_k, base_v, a_in, b_out, cache, generated, thm, live, apr, ppr, cnt):
+    H = lax.axis_size("hosts")
+    A, W = hidden.shape
+    capacity = A // H
+    fits = (
+        capacity == 8
+        and H <= 8
+        and A <= 128
+        and a_in.shape[0] == 1
+        and A * cache.shape[0] == 128
+        and cache.shape[2] == 128
+        and H * A == 128
+        and W == 8 * HEAD_SIZE
+        and generated.shape[2] == 8
+        and apr.shape[0] < 8
+    )
+    run = fused_body if fits else body
+    return run(hidden, base_q, base_k, base_v, a_in, b_out, cache, generated, thm, live, apr, ppr, cnt)
+
+
 def solution(mesh):
     placed = (
         P(("groups", "hosts"), "mp"),
@@ -258,7 +666,7 @@
         P("groups"),
     )
     return jax.shard_map(
-        body,
+        step,
         mesh=mesh,
         in_specs=placed,
         out_specs=(

time: 241 us -> 35.8 us (0.15)
  waiting for transfers between devices: 88.3 us -> 0 us
  starting transfers between devices: 85 us -> 0 us
  Pallas kernels: 0 us -> 29.8 us
  matrix products: 21.9 us -> 0 us
  local copies, waits for them, and re-layouts: 18 us -> 4.42 us
  other arithmetic: 12.8 us -> 0 us
  blocking collectives: 10.4 us -> 0 us
    all_to_all x23 -> x0, waiting for transfers between devices: 88.3 us -> none  [the longest x4 21.9 us: body(): lax.all_to_all(answer_mixed_rows, 'hosts', split_axis=0, concat_axis=0, t...]
    all_to_all x23 -> x0, starting transfers between devices: 85 us -> none  [the longest x4 14.9 us: body(): lax.all_to_all(request[2], 'hosts', split_axis=0, concat_axis=0, tiled=True)]
    pallas_call x0 -> x1, Pallas kernels: none -> 29.8 us  [fused_body(): pl.pallas_call(functools.partial(fused_kernel, sizes), out_shape=[jax.Sha...]
    dot_general x36 -> x0, matrix products: 21.9 us -> none  [the longest x10 6.59 us: pack_rows(): jnp.dot(router, payload, preferred_element_type=jnp.float32)]
    psum x1 -> x0, blocking collectives: 10.4 us -> none  [body(): rank_rows = lax.psum(partial_rank, 'mp').astype(jnp.bfloat16)]
    reshape x21 -> x0, local copies, waits for them, and re-layouts: 6.78 us -> none  [the longest x8 2.76 us: body(): pack_rows(router, block_pick).reshape(host_total, capacity, local_blocks)]
    reduce_sum x12 -> x0, other arithmetic: 5.01 us -> none  [the longest x4 2.38 us: attend_local(): totals = jnp.sum(weights, axis=(2, 4))]
    reduce_max x4 -> x0, local copies, waits for them, and re-layouts: 3.16 us -> none  [attend_local(): top_score = jnp.max(masked, axis=(2, 4))]
  transfers between devices with their start and end apart: 23 -> 0, of which waited for: 20 -> 0; matrix products, arithmetic and copies ran while one was open for 20% -> 0% of each run, Pallas kernels for 0% -> 0%
where the time goes in v1:
time: 35.8 us; the launch traced here: 35.5 us
  Pallas kernels  29.8 us (83%)
  local copies, waits for them, and re-layouts  4.42 us (12%)
  between operations  1.29 us (4%)
    pallas_call x1, Pallas kernels, fused_body(): pl.pallas_call(functools.partial(fused_kernel, sizes), out_shape=[jax.Sha...  29.8 us
    unnamed x3, local copies, waits for them, and re-layouts  4.42 us

profile of v1, /device:TPU:0, one launch (start us, length us, event | category | flops | bytes accessed | tf_op | source)
XLA Modules:
  0.0 35.5 jit_solution(8749080816881790635)
XLA Ops:
  1.3 29.8 %shard_map.148 = (bf16[32,1024]{1,0:T(8,128)(2,1)}, bf16[32,1024]{1,0:T(8,128)(2,1)}, bf16[32,1024]{1,0:T(8,128)(2,1)}) custom-call(s32[32]{0:T(128)} %thm.1, s32[1]{0:T(128)S(6)} %copy.19.live, s32[4]{0:T(128)} %apr.1, s32[4,4]{1,0:T(4,128)} %ppr.1, s32[4]{0:T(128)} %cnt.1, bf16[32,1024]{1,0:T(8,128)(2,1)} %hidden.1, bf16[32,1024]{1,0:T(8,128)(2,1)} %base_q.1, ...), custom_call_target="tpu_custom_call" | custom-call | flops 200000000 | bytes 4000000 | tf_op jit(solution)/shard_map/pallas_call | solution.py:594
  31.1 1.5 %copy.20 = bf16[32,1024]{1,0:T(8,128)(2,1)} copy(bf16[32,1024]{1,0:T(8,128)(2,1)} %get-tuple-element.6) | data formatting | bytes 131072
  32.5 1.5 %copy.21 = bf16[32,1024]{1,0:T(8,128)(2,1)} copy(bf16[32,1024]{1,0:T(8,128)(2,1)} %get-tuple-element.7) | data formatting | bytes 131072
  34.0 1.5 %copy.22 = bf16[32,1024]{1,0:T(8,128)(2,1)} copy(bf16[32,1024]{1,0:T(8,128)(2,1)} %get-tuple-element.8) | data formatting | bytes 131072

commit v2 on v1

--- a/solution.py
+++ b/solution.py
@@ -261,10 +261,10 @@
 
 def fused_kernel(
     sizes,
-    thm, live, apr, ppr, cnt,
-    hidden, base_q, base_k, base_v, a_hbm, b_hbm, kv_hbm, gen_hbm,
+    thm, apr, ppr, cnt,
+    hidden, base_q, live_hbm, k_hbm, val_hbm, a_hbm, b_hbm, kv_hbm, gen_hbm,
     out, key_out, val_out,
-    a_v, b_v, kv_v, gen_v,
+    live, base_k, base_v, a_v, b_v, kv_v, gen_v,
     snd_h, rcv_h, snd_q, rcv_q, part, snd_v, rcv_v, snd_m, rcv_m, snd_l, rcv_l, own_mix,
     local_sem, h_s, h_r, bq_s, bq_r, p_s, p_r, q_s, q_r, v_s, v_r, m_s, m_r, l_s, l_r,
     *queries,
@@ -286,11 +286,14 @@
     locals_ = [
         pltpu.make_async_copy(src, dst, local_sem.at[i])
         for i, (src, dst) in enumerate(
-            [(a_hbm, a_v), (b_hbm, b_v), (kv_hbm, kv_v), (gen_hbm, gen_v)]
+            [
+                (a_hbm, a_v), (b_hbm, b_v), (kv_hbm, kv_v), (gen_hbm, gen_v),
+                (live_hbm, live), (k_hbm, base_k), (val_hbm, base_v),
+            ]
         )
     ]
-    for copy in locals_:
-        copy.start()
+    for i in (4, 0, 1, 2, 5, 6, 3):
+        locals_[i].start()
 
     barrier = pltpu.get_barrier_semaphore()
     for d in range(1, H):
@@ -313,6 +316,7 @@
     owner = jnp.full((8, 128), -1, jnp.int32)
     for t in range(T):
         owner = jnp.where(th == t, apr[t], owner)
+    locals_[4].wait()
     n_live = live[0]
     owner = jnp.where(lane8 < n_live, owner, -1)
     member = jnp.where(owner == sub8, 1.0, 0.0).astype(f32)
@@ -445,6 +449,7 @@
         owner_c * CAP + rank_c == _iota((A, S), 1), jnp.where(owner_c >= 0, 1.0, 0.0), 0.0
     ).astype(bf)
     keys = []
+    locals_[5].wait()
     for h in range(HEADS):
         cols = slice(h * D, (h + 1) * D)
         key = turn(base_k[:, cols].astype(f32), cos_a, sin_a).astype(bf).astype(f32)
@@ -514,6 +519,7 @@
     rcv_m[me] = snd_m[me]
 
     locals_[3].wait()
+    locals_[6].wait()
     for copy in vs:
         copy.wait_recv()
     dv = rcv_v[...].astype(f32)
@@ -573,6 +579,15 @@
             copy.wait_send()
 
 
+def write_kernel(*refs):
+    sems = refs[6]
+    copies = [pltpu.make_async_copy(refs[i], refs[3 + i], sems.at[i]) for i in range(3)]
+    for copy in copies:
+        copy.start()
+    for copy in copies:
+        copy.wait()
+
+
 def fused_body(
     hidden, base_q, base_k, base_v, a_in, b_out, cache, generated, thm, live, apr, ppr, cnt
 ):
@@ -591,12 +606,15 @@
     hbm = pl.BlockSpec(memory_space=pl.ANY)
     fold = (H, 2 * CAP, W // 2)
     sem = lambda *shape: pltpu.SemaphoreType.DMA(shape)
-    return pl.pallas_call(
+    results = pl.pallas_call(
         functools.partial(fused_kernel, sizes),
-        out_shape=[jax.ShapeDtypeStruct((A, W), bf)] * 3,
-        in_specs=[smem] * 5 + [vmem] * 4 + [hbm] * 4,
+        out_shape=[pltpu.VMEM((A, W), bf)] * 3,
+        in_specs=[smem] * 4 + [vmem] * 2 + [hbm] * 7,
         out_specs=[vmem] * 3,
         scratch_shapes=[
+            pltpu.SMEM(live.shape, jnp.int32),
+            pltpu.VMEM((A, W), bf),
+            pltpu.VMEM((A, W), bf),
             pltpu.VMEM(a_in.shape, bf),
             pltpu.VMEM(b_out.shape, bf),
             pltpu.VMEM(cache.shape, bf),
@@ -613,7 +631,7 @@
             pltpu.VMEM((H, HEADS, 128), f32),
             pltpu.VMEM((H, HEADS, 128), f32),
             pltpu.VMEM((A, W), f32),
-            sem(4), sem(H), sem(H), sem(H), sem(H), sem(MP), sem(MP),
+            sem(7), sem(H), sem(H), sem(H), sem(H), sem(MP), sem(MP),
             sem(NCH, H), sem(NCH, H), sem(H), sem(H), sem(NCH, H), sem(NCH, H), sem(H), sem(H),
         ]
         + [pltpu.VMEM((H, S, W // NCH), bf)] * NCH,
@@ -624,9 +642,16 @@
             flops=2 * 10**8, bytes_accessed=4 * 10**6, transcendentals=10**6
         ),
     )(
-        thm, live, apr, ppr, cnt, hidden, base_q, base_k, base_v, a_in, b_out, cache,
+        thm, apr, ppr, cnt, hidden, base_q, live, base_k, base_v, a_in, b_out, cache,
         generated.reshape(N, W),
     )
+    return pl.pallas_call(
+        write_kernel,
+        out_shape=[jax.ShapeDtypeStruct((A, W), bf)] * 3,
+        in_specs=[vmem] * 3,
+        out_specs=[hbm] * 3,
+        scratch_shapes=[sem(3)],
+    )(*results)
 
 
 def step(hidden, base_q, base_k, base_v, a_in, b_out, cache, generated, thm, live, apr, ppr, cnt):

time: 35.8 us -> 34 us (0.950)
  local copies, waits for them, and re-layouts: 4.42 us -> 1.84 us
  Pallas kernels: 29.8 us -> 30.7 us
    unnamed x3 -> x6, local copies, waits for them, and re-layouts: 4.42 us -> 1.84 us
    pallas_call x1 -> x2, Pallas kernels: 29.8 us -> 30.7 us  [the longest x1 29.1 us: fused_body(): pl.pallas_call(functools.partial(fused_kernel, sizes), out_shape=[pltpu.V...]
where the time goes in v2:
time: 34 us; the launch traced here: 33.8 us
  Pallas kernels  30.7 us (90%)
  local copies, waits for them, and re-layouts  1.84 us (5%)
  between operations  1.3 us (4%)
    pallas_call x1, Pallas kernels, fused_body(): pl.pallas_call(functools.partial(fused_kernel, sizes), out_shape=[pltpu.V...  29.1 us
    unnamed x6, local copies, waits for them, and re-layouts  1.84 us
    pallas_call x1, Pallas kernels, fused_body(): pl.pallas_call(write_kernel, out_shape=[jax.ShapeDtypeStruct((A, W), bf)]...  1.6 us

profile of v2, /device:TPU:0, one launch (start us, length us, event | category | flops | bytes accessed | tf_op | source)
XLA Modules:
  0.0 33.8 jit_solution(11738359888495783746)
XLA Ops:
  1.3 29.1 %shard_map.148 = (bf16[32,1024]{1,0:T(8,128)(2,1)S(1)}, bf16[32,1024]{1,0:T(8,128)(2,1)S(1)}, bf16[32,1024]{1,0:T(8,128)(2,1)S(1)}) custom-call(s32[32]{0:T(128)} %thm.1, s32[4]{0:T(128)} %apr.1, s32[4,4]{1,0:T(4,128)} %ppr.1, s32[4]{0:T(128)} %cnt.1, bf16[32,1024]{1,0:T(8,128)(2,1)} %hidden.1, bf16[32,1024]{1,0:T(8,128)(2,1)} %base_q.1, ...), custom_call_target="tpu_custom_call" | custom-call | flops 200000000 | bytes 4000000 | tf_op jit(solution)/shard_map/pallas_call | solution.py:609
  30.4 0.0 copy-start
  30.4 0.6 %copy-done = bf16[32,1024]{1,0:T(8,128)(2,1)} copy-done((bf16[32,1024]{1,0:T(8,128)(2,1)}, bf16[32,1024]{1,0:T(8,128)(2,1)S(1)}, u32[]{:S(2)}) %copy-start) | copy-done | bytes 65560
  31.0 0.0 copy-start.1
  31.0 0.6 %copy-done.1 = bf16[32,1024]{1,0:T(8,128)(2,1)} copy-done((bf16[32,1024]{1,0:T(8,128)(2,1)}, bf16[32,1024]{1,0:T(8,128)(2,1)S(1)}, u32[]{:S(2)}) %copy-start.1) | copy-done | bytes 65560
  31.6 0.0 copy-start.2
  31.6 0.6 %copy-done.2 = bf16[32,1024]{1,0:T(8,128)(2,1)} copy-done((bf16[32,1024]{1,0:T(8,128)(2,1)}, bf16[32,1024]{1,0:T(8,128)(2,1)S(1)}, u32[]{:S(2)}) %copy-start.2) | copy-done | bytes 65560
  32.2 1.6 %shard_map.149 = (bf16[32,1024]{1,0:T(8,128)(2,1)}, bf16[32,1024]{1,0:T(8,128)(2,1)}, bf16[32,1024]{1,0:T(8,128)(2,1)}) custom-call(bf16[32,1024]{1,0:T(8,128)(2,1)} %copy-done, bf16[32,1024]{1,0:T(8,128)(2,1)} %copy-done.1, bf16[32,1024]{1,0:T(8,128)(2,1)} %copy-done.2), custom_call_target="tpu_custom_call" | custom-call | tf_op jit(solution)/shard_map/pallas_call | solution.py:648
Async XLA Ops:
  30.4 0.6 %copy-start = (bf16[32,1024]{1,0:T(8,128)(2,1)}, bf16[32,1024]{1,0:T(8,128)(2,1)S(1)}, u32[]{:S(2)}) copy-start(bf16[32,1024]{1,0:T(8,128)(2,1)S(1)} %get-tuple-element.6.refs_0_) | copy-start | bytes 196612
  31.0 0.6 %copy-start.1 = (bf16[32,1024]{1,0:T(8,128)(2,1)}, bf16[32,1024]{1,0:T(8,128)(2,1)S(1)}, u32[]{:S(2)}) copy-start(bf16[32,1024]{1,0:T(8,128)(2,1)S(1)} %get-tuple-element.7.refs_1_) | copy-start | bytes 196612
  31.6 0.6 %copy-start.2 = (bf16[32,1024]{1,0:T(8,128)(2,1)}, bf16[32,1024]{1,0:T(8,128)(2,1)S(1)}, u32[]{:S(2)}) copy-start(bf16[32,1024]{1,0:T(8,128)(2,1)S(1)} %get-tuple-element.8.refs_2_) | copy-start | bytes 196612

commit v3 on v2

--- a/solution.py
+++ b/solution.py
@@ -519,26 +519,12 @@
     rcv_m[me] = snd_m[me]
 
     locals_[3].wait()
-    locals_[6].wait()
-    for copy in vs:
-        copy.wait_recv()
-    dv = rcv_v[...].astype(f32)
-    dv_att = [
-        _dot(
-            unpack,
-            jnp.concatenate([dv[p, k * CAP : (k + 1) * CAP] for p in range(H)], axis=0).astype(bf),
-        )
-        for k in range(2)
-    ]
     N = gen_v.shape[0]
     lane_n, sub_n = _iota((A, N), 1), _iota((A, N), 0)
     mine = ((lane_n >> (SUF.bit_length())) == sub_n) & ((lane_n & (2 * SUF - 1)) < SUF)
-    own_top, own_total = [], []
+    own_top, own_total, own_self = [], [], []
     for h in range(HEADS):
         cols = slice(h * D, (h + 1) * D)
-        k, off = (h * D) // W2, (h * D) % W2
-        value = (base_v[:, cols].astype(f32) + dv_att[k][:, off : off + D]).astype(bf).astype(f32)
-        val_out[:, cols] = jnp.where(live_c, value, 0.0).astype(bf)
         c, start = (h * D) // CW, (h * D) % CW
         query = _dot(fetch, queries[c][:, :, start : start + D].reshape(H * S, D))
         scores = _dot_t(query.astype(bf), gen_v[:, cols]) * scale
@@ -551,8 +537,26 @@
         own_total.append(jnp.sum(weights, axis=1, keepdims=True) + self_weight)
         own_mix[:, cols] = (
             _dot(pltpu.roll(weights, SUF, 1).astype(bf), gen_v[:, cols])
-            + self_weight.astype(bf).astype(f32) * value
-        )
+        )
+        own_self.append(self_weight.astype(bf).astype(f32))
+
+    locals_[6].wait()
+    for copy in vs:
+        copy.wait_recv()
+    dv = rcv_v[...].astype(f32)
+    dv_att = [
+        _dot(
+            unpack,
+            jnp.concatenate([dv[p, k * CAP : (k + 1) * CAP] for p in range(H)], axis=0).astype(bf),
+        )
+        for k in range(2)
+    ]
+    for h in range(HEADS):
+        cols = slice(h * D, (h + 1) * D)
+        k, off = (h * D) // W2, (h * D) % W2
+        value = (base_v[:, cols].astype(f32) + dv_att[k][:, off : off + D]).astype(bf).astype(f32)
+        val_out[:, cols] = jnp.where(live_c, value, 0.0).astype(bf)
+        own_mix[:, cols] += own_self[h] * value
 
     for copy in ls:
         copy.wait_recv()
@@ -651,6 +655,7 @@
         in_specs=[vmem] * 3,
         out_specs=[hbm] * 3,
         scratch_shapes=[sem(3)],
+        compiler_params=pltpu.CompilerParams(vmem_limit_bytes=2**20),
     )(*results)
 
 

time: 34 us -> 31.2 us (0.918)
  local copies, waits for them, and re-layouts: 1.84 us -> 0 us
  Pallas kernels: 30.7 us -> 29.8 us
    unnamed x6 -> x0, local copies, waits for them, and re-layouts: 1.84 us -> none
    pallas_call x1, Pallas kernels: 1.6 us -> 0.7 us  [fused_body(): pl.pallas_call(write_kernel, out_shape=[jax.ShapeDtypeStruct((A, W), bf)]...]
where the time goes in v3:
time: 31.2 us; the launch traced here: 31.1 us
  Pallas kernels  29.8 us (96%)
  between operations  1.29 us (4%)
    pallas_call x1, Pallas kernels, fused_body(): pl.pallas_call(functools.partial(fused_kernel, sizes), out_shape=[pltpu.V...  29.1 us
    pallas_call x1, Pallas kernels, fused_body(): pl.pallas_call(write_kernel, out_shape=[jax.ShapeDtypeStruct((A, W), bf)]...  0.7 us

profile of v3, /device:TPU:0, one launch (start us, length us, event | category | flops | bytes accessed | tf_op | source)
XLA Modules:
  0.0 31.1 jit_solution(2778566724616222457)
XLA Ops:
  1.3 29.1 %shard_map.148 = (bf16[32,1024]{1,0:T(8,128)(2,1)S(1)}, bf16[32,1024]{1,0:T(8,128)(2,1)S(1)}, bf16[32,1024]{1,0:T(8,128)(2,1)S(1)}) custom-call(s32[32]{0:T(128)} %thm.1, s32[4]{0:T(128)} %apr.1, s32[4,4]{1,0:T(4,128)} %ppr.1, s32[4]{0:T(128)} %cnt.1, bf16[32,1024]{1,0:T(8,128)(2,1)} %hidden.1, bf16[32,1024]{1,0:T(8,128)(2,1)} %base_q.1, ...), custom_call_target="tpu_custom_call" | custom-call | flops 200000000 | bytes 4000000 | tf_op jit(solution)/shard_map/pallas_call | solution.py:613
  30.4 0.7 %shard_map.149 = (bf16[32,1024]{1,0:T(8,128)(2,1)}, bf16[32,1024]{1,0:T(8,128)(2,1)}, bf16[32,1024]{1,0:T(8,128)(2,1)}) custom-call(bf16[32,1024]{1,0:T(8,128)(2,1)S(1)} %get-tuple-element.6.refs_0_, bf16[32,1024]{1,0:T(8,128)(2,1)S(1)} %get-tuple-element.7.refs_1_, bf16[32,1024]{1,0:T(8,128)(2,1)S(1)} %get-tuple-element.8.refs_2_), custom_call_target="tpu_custom_call" | custom-call | tf_op jit(solution)/shard_map/pallas_call | solution.py:652

commit v4 on v3

--- a/solution.py
+++ b/solution.py
@@ -465,8 +465,9 @@
         whose.append(index)
     scale = D ** (-0.5)
     locals_[2].wait()
-    lane128 = _iota((128, 128), 1)
-    lse_all = jnp.zeros((128, 128), f32)
+    lane_block = (_iota((128, 128), 1) >> shift) & (L - 1)
+    sub_h = _iota((HEADS, 128), 0)
+    lse_t = jnp.zeros((HEADS, 128), f32)
     ms = []
     for c in range(NCH):
         for copy in qs[c]:
@@ -474,31 +475,30 @@
         for h in range(c * CW // D, (c + 1) * CW // D):
             cols = slice(h * D, (h + 1) * D)
             within = slice(h * D - c * CW, (h + 1) * D - c * CW)
-            scores = jnp.concatenate(
-                [_dot_t(queries[c][whose[b], :, within], kv_v[b, 0, :, cols]) for b in range(L)], axis=0
-            ) * scale
-            top = jnp.max(scores, axis=1, keepdims=True)
+            asked = [queries[c][whose[b], :, within].astype(f32) for b in range(L)]
+            asked = jnp.concatenate(
+                [asked[b][e * CAP : (e + 1) * CAP] for e in range(H) for b in range(L)], axis=0
+            ).astype(bf)
+            scores = _dot_t(kv_v[0, 0, :, cols], asked)
+            for b in range(1, L):
+                scores = jnp.where(lane_block == b, _dot_t(kv_v[b, 0, :, cols], asked), scores)
+            scores = scores * scale
+            top = jnp.max(scores, axis=0, keepdims=True)
             weights = jnp.exp(scores - top)
-            total = jnp.sum(weights, axis=1, keepdims=True)
-            weights = weights.astype(bf)
-            mixed = jnp.concatenate(
-                [_dot(weights[b * S : (b + 1) * S], kv_v[b, 1, :, cols]) for b in range(L)], axis=0
-            ) * (1.0 / total)
-            lse_all = jnp.where(lane128 == h, top + jnp.log(total), lse_all)
+            total = jnp.sum(weights, axis=0, keepdims=True)
+            lse_t = jnp.where(sub_h == h, top + jnp.log(total), lse_t)
+            weights = (weights * (1.0 / total)).T
+            mixed = []
+            for b in range(L):
+                rows = jnp.concatenate(
+                    [weights[(e * L + b) * CAP : (e * L + b + 1) * CAP] for e in range(H)], axis=0
+                )
+                mixed.append(_dot(rows.astype(bf), kv_v[b, 1, :, cols]))
             for e in range(H):
                 snd_m[e, :, cols] = jnp.concatenate(
-                    [mixed[b * S + e * CAP : b * S + (e + 1) * CAP] for b in range(L)], axis=0
+                    [mixed[b][e * CAP : (e + 1) * CAP] for b in range(L)], axis=0
                 ).astype(bf)
         if c == NCH - 1:
-            ordered = jnp.concatenate(
-                [
-                    lse_all[b * S + e * CAP : b * S + (e + 1) * CAP]
-                    for e in range(H)
-                    for b in range(L)
-                ],
-                axis=0,
-            )
-            lse_t = ordered.T[:HEADS]
             rcv_l[me] = lse_t
             for d in range(1, H):
                 snd_l[d] = pltpu.roll(lse_t, (128 - L * CAP * d) % 128, 1)
@@ -669,6 +669,7 @@
         and A <= 128
         and a_in.shape[0] == 1
         and A * cache.shape[0] == 128
+        and cache.shape[0] == 4
         and cache.shape[2] == 128
         and H * A == 128
         and W == 8 * HEAD_SIZE

time: 31.2 us -> 31.2 us (level)
  no operation moved by 1% of the time
where the time goes in v4:
time: 31.2 us; the launch traced here: 31.1 us
  Pallas kernels  29.8 us (96%)
  between operations  1.29 us (4%)
    pallas_call x1, Pallas kernels, fused_body(): pl.pallas_call(functools.partial(fused_kernel, sizes), out_shape=[pltpu.V...  29.1 us
    pallas_call x1, Pallas kernels, fused_body(): pl.pallas_call(write_kernel, out_shape=[jax.ShapeDtypeStruct((A, W), bf)]...  0.7 us

profile of v4, /device:TPU:0, one launch (start us, length us, event | category | flops | bytes accessed | tf_op | source)
XLA Modules:
  0.0 31.1 jit_solution(5189860871640295572)
XLA Ops:
  1.3 29.1 %shard_map.148 = (bf16[32,1024]{1,0:T(8,128)(2,1)S(1)}, bf16[32,1024]{1,0:T(8,128)(2,1)S(1)}, bf16[32,1024]{1,0:T(8,128)(2,1)S(1)}) custom-call(s32[32]{0:T(128)} %thm.1, s32[4]{0:T(128)} %apr.1, s32[4,4]{1,0:T(4,128)} %ppr.1, s32[4]{0:T(128)} %cnt.1, bf16[32,1024]{1,0:T(8,128)(2,1)} %hidden.1, bf16[32,1024]{1,0:T(8,128)(2,1)} %base_q.1, ...), custom_call_target="tpu_custom_call" | custom-call | flops 200000000 | bytes 4000000 | tf_op jit(solution)/shard_map/pallas_call | solution.py:613
  30.4 0.7 %shard_map.149 = (bf16[32,1024]{1,0:T(8,128)(2,1)}, bf16[32,1024]{1,0:T(8,128)(2,1)}, bf16[32,1024]{1,0:T(8,128)(2,1)}) custom-call(bf16[32,1024]{1,0:T(8,128)(2,1)S(1)} %get-tuple-element.6.refs_0_, bf16[32,1024]{1,0:T(8,128)(2,1)S(1)} %get-tuple-element.7.refs_1_, bf16[32,1024]{1,0:T(8,128)(2,1)S(1)} %get-tuple-element.8.refs_2_), custom_call_target="tpu_custom_call" | custom-call | tf_op jit(solution)/shard_map/pallas_call | solution.py:652

commit v5 on v4

--- a/solution.py
+++ b/solution.py
@@ -601,7 +601,7 @@
     L, SUF = cache.shape[0], generated.shape[2]
     HEADS = W // HEAD_SIZE
     S = H * CAP
-    NCH = 2
+    NCH = 4
     bf, f32 = jnp.bfloat16, jnp.float32
     N = generated.shape[0] * 2 * SUF
     sizes = (H, MP, A, CAP, L, apr.shape[0], ppr.shape[1], HEADS, SUF, NCH)

time: 31.2 us -> 32.1 us (1.029)
  Pallas kernels: 29.8 us -> 30.6 us
    pallas_call x1, Pallas kernels: 29.1 us -> 29.9 us  [fused_body(): pl.pallas_call(functools.partial(fused_kernel, sizes), out_shape=[pltpu.V...]
where the time goes in v5:
time: 32.1 us; the launch traced here: 31.9 us
  Pallas kernels  30.6 us (95%)
  between operations  1.29 us (4%)
    pallas_call x1, Pallas kernels, fused_body(): pl.pallas_call(functools.partial(fused_kernel, sizes), out_shape=[pltpu.V...  29.9 us
    pallas_call x1, Pallas kernels, fused_body(): pl.pallas_call(write_kernel, out_shape=[jax.ShapeDtypeStruct((A, W), bf)]...  0.7 us

profile of v5, /device:TPU:0, one launch (start us, length us, event | category | flops | bytes accessed | tf_op | source)
XLA Modules:
  0.0 31.9 jit_solution(7508356470238560788)
XLA Ops:
  1.3 29.9 %shard_map.148 = (bf16[32,1024]{1,0:T(8,128)(2,1)S(1)}, bf16[32,1024]{1,0:T(8,128)(2,1)S(1)}, bf16[32,1024]{1,0:T(8,128)(2,1)S(1)}) custom-call(s32[32]{0:T(128)} %thm.1, s32[4]{0:T(128)} %apr.1, s32[4,4]{1,0:T(4,128)} %ppr.1, s32[4]{0:T(128)} %cnt.1, bf16[32,1024]{1,0:T(8,128)(2,1)} %hidden.1, bf16[32,1024]{1,0:T(8,128)(2,1)} %base_q.1, ...), custom_call_target="tpu_custom_call" | custom-call | flops 200000000 | bytes 4000000 | tf_op jit(solution)/shard_map/pallas_call | solution.py:613
  31.2 0.7 %shard_map.149 = (bf16[32,1024]{1,0:T(8,128)(2,1)}, bf16[32,1024]{1,0:T(8,128)(2,1)}, bf16[32,1024]{1,0:T(8,128)(2,1)}) custom-call(bf16[32,1024]{1,0:T(8,128)(2,1)S(1)} %get-tuple-element.6.refs_0_, bf16[32,1024]{1,0:T(8,128)(2,1)S(1)} %get-tuple-element.7.refs_1_, bf16[32,1024]{1,0:T(8,128)(2,1)S(1)} %get-tuple-element.8.refs_2_), custom_call_target="tpu_custom_call" | custom-call | tf_op jit(solution)/shard_map/pallas_call | solution.py:652
